TPU v7x, 32 devices: a whole 2x2x4 slice. The times are simulated.
32 devices in a mesh: station: 32 (over z, y, x, core), sample: 1.
Axes of the slice: x: 2, y: 2, z: 4, core: 2. Of those that a mesh axis runs over, the one named last changes fastest.
Arguments:
- flux: bfloat16 [4, 1024, 3584], P('sample', 'station'), may hold values from -6 to 6
- coeff: float32 [1024, 3584], P('station'), may hold values from 0.02 to 0.24
- diff_steps: int32 [4], P('sample'), may hold values from 3 to 6, as said below
- footprint: bfloat16 [512, 4, 16384], P('station'), may hold values from -0.03125 to 0.03125
- tile_src: int32 [512, 4, 1], replicated, may hold values from 0 to 31; in each aligned block of 64 rows (0 to 63, 64 to 127, ..., all dimensions but the last counted through in order) at most 4 rows name the same one
- tile_local: int32 [512, 4], replicated, may hold values from 0 to 6
- tile_count: int32 [512], P('station'), may hold values from 1 to 4
Outputs:
- observed: float32 [512, 4], P('station')
Inputs may be any that keep to these rules, and one draw needn't show every extreme that they name: `tile_src`: in each aligned block of 64 rows (the slots of one index's stations, stations and slots in order), no band appears more than 4 times, and some band appears exactly 4 times. `diff_steps`: some sample takes 6 steps and another takes 3.
All inputs are finite; a program needn't handle non-finite values.
Results may differ from a plain program's by a relative error of at most 0.0029.
Values may be sent and summed in bfloat16 or wider, within the bound.
A program may use at most 128 MiB of HBM per device.

v0:
```python
import functools

import jax
import jax.numpy as jnp
from jax import lax
from jax.experimental import pallas as pl
from jax.experimental.pallas import tpu as pltpu
from jax.sharding import PartitionSpec as P

TILE_LON = 512
TILES_DEV = 7
LANES_T = 8
KT = 4
ITERS = 6
INNER = 8
PIECES = 8
GROUP_ROWS = 16
MESH = pl.DeviceIdType.MESH


def east_west(x, lane, tile):
    width = x.shape[1]
    west = pltpu.roll(x, 1, 1)
    first = west[:, :128]
    before = jnp.where(tile == 0, pltpu.roll(first, 2, 0), pltpu.roll(first, 1, 0))
    first = jnp.where(lane == 0, before, first)
    west = jnp.concatenate([first, west[:, 128:]], axis=1)
    east = pltpu.roll(x, width - 1, 1)
    last = east[:, width - 128 :]
    after = jnp.where(tile == TILES_DEV - 1, pltpu.roll(last, 6, 0), pltpu.roll(last, 7, 0))
    last = jnp.where(lane == 127, after, last)
    east = jnp.concatenate([east[:, : width - 128], last], axis=1)
    return west, east


def kernel(
    outer_n, slots, splits,
    steps, prints, hot, hot2, flux, coef, sel, sel2, group, weights, weights2,
    out,
    send, arr, send2, arr2, halo_f, halo_c, field_a, field_b, cof, tiles, acc, val, ret, val2, ret2,
    f_send, f_recv, g_send, g_recv, h_send, h_recv, r_send, r_recv, l_send, l_recv, v_send, v_recv, w_send, w_recv,
):
    rows = flux.shape[0]
    wide = flux.shape[1]
    samples = wide // LANES_T
    count = outer_n * INNER
    me = lax.axis_index("station")
    outer, inner = me // INNER, lax.rem(me, INNER)
    base = outer * INNER
    has_up, has_down = me > 0, me < count - 1
    has_left, has_right = outer > 0, outer < outer_n - 1
    first, last = outer == 0, outer == outer_n - 1
    is_end = jnp.logical_or(first, last)
    is_next = jnp.logical_or(outer == 1, outer == outer_n - 2)
    other_base = jnp.where(first, 1, jnp.where(last, outer_n - 2, jnp.where(outer == 1, 0, outer_n - 1))) * INNER
    lone_left = jnp.logical_and(outer >= 2, outer <= outer_n - 2)
    lone_right = jnp.logical_and(outer >= 1, outer <= outer_n - 3)
    lone_up = jnp.logical_and(lone_left, inner == 0)
    lone_down = jnp.logical_and(lone_right, inner == INNER - 1)

    def peer(offset):
        return base + lax.rem(inner + offset, INNER)

    def across(offset):
        return other_base + lax.rem(inner + offset, INNER)

    barrier = pltpu.get_barrier_semaphore()

    def greet(device):
        pl.semaphore_signal(barrier, inc=1, device_id={"station": device}, device_id_type=MESH)

    for offset in range(1, INNER):
        greet(peer(offset))
    others = ((lone_left, -INNER), (lone_right, INNER), (lone_up, -1), (lone_down, 1))
    for there, step in others:
        @pl.when(there)
        def _():
            greet(me + step)

    paired = jnp.logical_or(is_end, is_next)

    @pl.when(paired)
    def _():
        for offset in range(INNER):
            greet(across(offset))
    pl.semaphore_wait(
        barrier,
        INNER - 1 + sum(jnp.where(there, 1, 0) for there, _ in others) + jnp.where(paired, INNER, 0),
    )

    def remote(src, dst, ssem, rsem, device):
        return pltpu.make_async_remote_copy(
            src_ref=src, dst_ref=dst, send_sem=ssem, recv_sem=rsem,
            device_id={"station": device}, device_id_type=MESH,
        )

    def halo_copies(way):
        step = -1 if way == 0 else 1
        cut = pl.ds(0, ITERS) if way == 0 else pl.ds(rows - ITERS, ITERS)
        return (
            remote(flux.at[cut], halo_f.at[1 - way], h_send.at[way, 0], h_recv.at[1 - way, 0], me + step),
            remote(coef.at[cut], halo_c.at[1 - way], h_send.at[way, 1], h_recv.at[1 - way, 1], me + step),
        )

    for way, there in ((0, has_up), (1, has_down)):
        @pl.when(there)
        def _():
            for copy in halo_copies(way):
                copy.start()

        @pl.when(jnp.logical_not(there))
        def _():
            halo_f[way] = jnp.zeros(halo_f.shape[1:], halo_f.dtype)
            halo_c[way] = jnp.zeros(halo_c.shape[1:], halo_c.dtype)

    cells = prints.shape[2]
    short = cells // splits

    def some_prints(at):
        block = prints[:, :, pl.ds(pl.multiple_of(at, 256), 256)]
        return block.reshape(block.shape[0] * KT, 256)

    own2 = pl.ds(pl.multiple_of(inner * GROUP_ROWS, GROUP_ROWS), GROUP_ROWS)

    def rows2(offset):
        return pl.ds(pl.multiple_of(lax.rem(inner + offset, INNER) * GROUP_ROWS, GROUP_ROWS), GROUP_ROWS)

    def group_copy(offset):
        return remote(send2.at[rows2(offset)], arr2.at[own2], g_send.at[offset], g_recv.at[offset], across(offset))

    @pl.when(is_end)
    def _():
        def pack2(i, carry):
            for j in range(2):
                at = i * 512 + j * 256
                stack = [some_prints(q * short + at) for q in range(splits)]
                packed = jnp.dot(hot2[...], jnp.concatenate(stack, axis=0), preferred_element_type=jnp.float32)
                send2[:, pl.ds(pl.multiple_of(at, 256), 256)] = packed.astype(jnp.bfloat16)
            return carry

        lax.fori_loop(0, short // 512, pack2, 0)
        for offset in range(INNER):
            group_copy(offset).start()
        missing = jnp.where(first, 1, outer_n - 2)

        def clear(r, carry):
            tiles[r, pl.ds(pl.multiple_of(missing * wide, wide), wide), :] = jnp.zeros((wide, TILE_LON), jnp.bfloat16)
            return carry

        lax.fori_loop(0, rows, clear, 0)

    length = cells // PIECES

    def print_copy(offset, c):
        target = peer(offset)
        lanes = pl.ds(pl.multiple_of(c * length, length), length)
        to_rows = pl.ds(pl.multiple_of(lax.rem(inner + offset, INNER) * slots, slots), slots)
        my_rows = pl.ds(pl.multiple_of(inner * slots, slots), slots)
        return remote(send.at[to_rows, lanes], arr.at[my_rows, lanes], f_send.at[offset, c], f_recv.at[offset, c], target)

    own = pl.ds(pl.multiple_of(inner * slots, slots), slots)

    def send_prints(c):
        for j in range(length // 256):
            at = c * length + j * 256
            packed = jnp.dot(hot[...], some_prints(at), preferred_element_type=jnp.float32)
            send[:, pl.ds(pl.multiple_of(at, 256), 256)] = packed.astype(jnp.bfloat16)
        for offset in range(1, INNER):
            print_copy(offset, c).start()

    def load(r, carry):
        field_a[r + ITERS] = flux[r].astype(jnp.float32)
        cof[r + ITERS] = coef[r]
        return carry

    lax.fori_loop(0, rows, load, 0)
    for way, there in ((0, has_up), (1, has_down)):
        @pl.when(there)
        def _():
            for copy in halo_copies(way):
                copy.wait_send()
            remote(flux.at[pl.ds(0, ITERS)], halo_f.at[way], h_send.at[way, 0], h_recv.at[way, 0], me).wait_recv()
            remote(coef.at[pl.ds(0, ITERS)], halo_c.at[way], h_send.at[way, 1], h_recv.at[way, 1], me).wait_recv()

    def load_halo(r, carry):
        field_a[r] = halo_f[0, r].astype(jnp.float32)
        cof[r] = halo_c[0, r]
        field_a[r + ITERS + rows] = halo_f[1, r].astype(jnp.float32)
        cof[r + ITERS + rows] = halo_c[1, r]
        return carry

    lax.fori_loop(0, ITERS, load_halo, 0)

    lane = lax.broadcasted_iota(jnp.int32, (LANES_T, 128), 1)
    tile = lax.broadcasted_iota(jnp.int32, (LANES_T, 128), 0)

    def updated(src, r, k, s):
        cut = slice(s * LANES_T, (s + 1) * LANES_T)
        center = src[r, cut, :]
        west, east = east_west(center, lane, tile)
        lap = src[r - 1, cut, :] + src[r + 1, cut, :] + west + east - 4.0 * center
        return center + jnp.where(k < steps[s], 1.0, 0.0) * cof[r] * lap

    piece = rows // PIECES

    def block_copy(block, c, k, to_right):
        at = tiles.at[pl.ds(c * piece, piece), pl.ds(pl.multiple_of(block * wide, wide), wide), :]
        if to_right:
            return remote(at, at, r_send.at[k, c], r_recv.at[k, c], me + INNER)
        return remote(at, at, l_send.at[k, c], l_recv.at[k, c], me - INNER)

    def goes(there, k, to_right):
        there = jnp.logical_and(there, has_right if to_right else has_left)
        if k == 0:
            there = jnp.logical_and(there, outer != (outer_n - 2 if to_right else 1))
        return there

    def start_block(block, c, k, to_right, there):
        @pl.when(goes(there, k, to_right))
        def _():
            block_copy(block, c, k, to_right).start()

    mine = pl.ds(pl.multiple_of(outer * wide, wide), wide)

    def step_row(r, k):
        src, dst = (field_a, field_b) if k % 2 == 0 else (field_b, field_a)
        done = [updated(src, r, k, s) for s in range(samples)]
        if k == ITERS - 1:
            tiles[r - ITERS, mine, :] = jnp.concatenate(done, axis=0).astype(jnp.bfloat16)
        else:
            for s in range(samples):
                dst[r, s * LANES_T : (s + 1) * LANES_T, :] = done[s]

    def send_piece(c):
        start_block(outer, c, 0, True, has_right)
        start_block(outer, c, 0, False, has_left)

    for k in range(ITERS):
        def row_pair(i, carry, k=k):
            step_row(k + 1 + 2 * i, k)
            step_row(k + 2 + 2 * i, k)
            return carry

        lax.fori_loop(0, piece // 2 + ITERS - 1 - k, row_pair, 0)
    send_piece(0)
    send_prints(0)

    def reach(k):
        from_left, from_right = outer - 1 - k >= 0, outer + 1 + k < outer_n
        if k == 0:
            from_left = jnp.logical_and(from_left, jnp.logical_not(last))
            from_right = jnp.logical_and(from_right, jnp.logical_not(first))
        return from_left, from_right

    def relay(c, k, begun=True):
        from_left, from_right = (jnp.logical_and(there, begun) for there in reach(k))

        @pl.when(from_left)
        def _():
            block_copy(outer - 1 - k, c, k, True).wait_recv()

        if k < outer_n - 2:
            start_block(outer - 1 - k, c, k + 1, True, from_left)

        @pl.when(from_right)
        def _():
            block_copy(outer + 1 + k, c, k, False).wait_recv()

        if k < outer_n - 2:
            start_block(outer + 1 + k, c, k + 1, False, from_right)

    def next_piece(c, carry):
        for k in range(ITERS):
            for j in range(piece):
                step_row(c * piece + 2 * ITERS - 1 - k + j, k)
        send_piece(c)
        relay(c - 1, 0)
        relay(c - 2, 1, c >= 2)
        send_prints(c)
        return carry

    lax.fori_loop(1, PIECES, next_piece, 0)
    relay(PIECES - 1, 0)
    relay(PIECES - 2, 1)
    relay(PIECES - 1, 1)
    arr[own, :] = send[own, :]

    def multiply(c):
        for offset in range(1, INNER):
            print_copy(offset, c).wait_recv()
        total = jnp.zeros(acc.shape, jnp.float32) if c == 0 else acc[...]
        for r in range(c * piece, (c + 1) * piece):
            total = total + lax.dot_general(
                arr[:, r * TILE_LON : (r + 1) * TILE_LON], tiles[r], (((1,), (1,)), ((), ())),
                preferred_element_type=jnp.float32,
            )
        acc[...] = total

    def value_copy2(offset):
        return remote(val2.at[rows2(offset)], ret2.at[own2], w_send.at[offset], w_recv.at[offset], across(offset))

    def group_values():
        for offset in range(INNER):
            group_copy(offset).wait_recv()
        per_split = rows // splits
        total = jnp.zeros(sel2.shape[1:], jnp.float32)
        for q in range(splits):
            def add_row(r, part, q=q):
                return part + lax.dot_general(
                    arr2[:, pl.ds(pl.multiple_of(r * TILE_LON, TILE_LON), TILE_LON)],
                    tiles[q * per_split + r, mine, :], (((1,), (1,)), ((), ())),
                    preferred_element_type=jnp.float32,
                )

            part = jnp.zeros(sel2.shape[1:], jnp.float32)
            for r in range(per_split):
                part = add_row(r, part)
            total = total + part * sel2[q]
        val2[...] = jnp.dot(total, group[:wide, :], precision=lax.Precision.HIGHEST, preferred_element_type=jnp.float32)
        for offset in range(INNER):
            value_copy2(offset).start()

    pl.when(is_next)(group_values)
    for k in range(2, outer_n - 1):
        for c in range(PIECES):
            relay(c, k)
            if k == outer_n - 2:
                multiply(c)

    val[...] = jnp.dot(acc[...] * sel[...], group[...], precision=lax.Precision.HIGHEST, preferred_element_type=jnp.float32)

    def value_copy(offset):
        to_rows = pl.ds(pl.multiple_of(lax.rem(inner + offset, INNER) * slots, slots), slots)
        return remote(val.at[to_rows], ret.at[own], v_send.at[offset], v_recv.at[offset], peer(offset))

    for offset in range(1, INNER):
        value_copy(offset).start()
    ret[own, :] = val[own, :]
    for offset in range(1, INNER):
        value_copy(offset).wait_recv()
    out[...] = jnp.dot(weights[...], ret[...], precision=lax.Precision.HIGHEST, preferred_element_type=jnp.float32)

    @pl.when(is_end)
    def _():
        for offset in range(INNER):
            value_copy2(offset).wait_recv()
        out[...] += jnp.dot(weights2[...], ret2[...], precision=lax.Precision.HIGHEST, preferred_element_type=jnp.float32)
        for offset in range(INNER):
            group_copy(offset).wait_send()

    @pl.when(is_next)
    def _():
        for offset in range(INNER):
            value_copy2(offset).wait_send()

    for offset in range(1, INNER):
        value_copy(offset).wait_send()
        for c in range(PIECES):
            print_copy(offset, c).wait_send()
    for k in range(outer_n - 1):
        for c in range(PIECES):
            @pl.when(goes(outer - k >= 0, k, True))
            def _():
                block_copy(outer - k, c, k, True).wait_send()

            @pl.when(goes(outer + k < outer_n, k, False))
            def _():
                block_copy(outer + k, c, k, False).wait_send()


def body(flux, coeff, diff_steps, footprint, tile_src, tile_local, tile_count):
    samples, rows, _ = flux.shape
    stations = footprint.shape[0]
    devices = lax.axis_size("station")
    outer_n = devices // INNER
    me = lax.axis_index("station")
    outer, inner = me // INNER, me % INNER
    slot_count = stations * KT
    cap = 2 * max(1, (slot_count + devices - 1) // devices)
    slots = outer_n * cap
    wide = samples * LANES_T

    flux_t = flux.reshape(samples, rows, TILES_DEV, TILE_LON).transpose(1, 0, 2, 3)
    flux_t = jnp.pad(flux_t, ((0, 0), (0, 0), (0, 1), (0, 0))).reshape(rows, wide, TILE_LON)
    coef_t = jnp.pad(coeff.reshape(rows, TILES_DEV, TILE_LON), ((0, 0), (0, 1), (0, 0)))

    order = jnp.arange(slot_count, dtype=jnp.int32)
    listed = (tile_src[:, :, 0] * LANES_T + tile_local).reshape(devices, slot_count)
    here = lax.dynamic_slice_in_dim(listed, outer * INNER, INNER, 0)
    src, loc = here // LANES_T, here % LANES_T
    target = src % INNER
    band_layer = src // INNER
    beside = jnp.where(outer == 0, 1, jnp.where(outer == outer_n - 1, outer_n - 2, -1))
    grouped = band_layer == beside
    target = jnp.where(grouped, INNER + target, target)
    same = (target[:, :, None] == target[:, None, :]) & (order[None, :] < order[:, None])[None]
    rank = jnp.sum(same.astype(jnp.int32), axis=2)
    places = jnp.arange(slots, dtype=jnp.int32)
    my_target = lax.dynamic_index_in_dim(target, inner, 0, keepdims=False)
    my_rank = lax.dynamic_index_in_dim(rank, inner, 0, keepdims=False)
    place = jnp.where(my_target < INNER, my_target * slots + my_rank, -1)
    hot = place[None, :] == jnp.arange(INNER * slots, dtype=jnp.int32)[:, None]
    splits = GROUP_ROWS // cap
    group_rows = jnp.arange(INNER * GROUP_ROWS, dtype=jnp.int32)
    row_owner, row_split, row_slot = group_rows // GROUP_ROWS, group_rows % GROUP_ROWS // cap, group_rows % cap
    in_group = (my_target[None, :] == INNER + row_owner[:, None]) & (my_rank[None, :] == row_slot[:, None])
    hot2 = in_group[:, None, :] & (row_split[:, None] == jnp.arange(splits, dtype=jnp.int32)[None, :])[:, :, None]
    hot2 = hot2.reshape(INNER * GROUP_ROWS, splits * slot_count)
    from_layer = jnp.where(outer == 1, 0, outer_n - 1)
    there = lax.dynamic_slice_in_dim(listed, from_layer * INNER, INNER, 0)
    src_end, loc_end = there // LANES_T, there % LANES_T
    to_me = src_end == me
    rank_end = jnp.sum((to_me[:, None, :] & (order[None, :] < order[:, None])[None]).astype(jnp.int32), axis=2)
    taken = to_me[:, None, :] & (rank_end[:, None, :] == jnp.arange(cap, dtype=jnp.int32)[None, :, None])
    tile_end = jnp.sum(jnp.where(taken, loc_end[:, None, :] + 1, 0), axis=2) - 1
    tile_end = jnp.broadcast_to(tile_end[:, None, :], (INNER, splits, cap)).reshape(INNER * GROUP_ROWS)
    sel2 = (tile_end[None, :, None] == (jnp.arange(wide, dtype=jnp.int32) % LANES_T)[None, None, :]) & (
        row_split[None, :, None] == jnp.arange(splits, dtype=jnp.int32)[:, None, None]
    )
    chosen = (target[:, None, :] == inner) & (rank[:, None, :] == places[None, :, None])
    code = band_layer * LANES_T + loc + 1
    named = jnp.sum(jnp.where(chosen, code[:, None, :], 0), axis=2).reshape(INNER * slots) - 1
    columns = jnp.arange(outer_n * wide, dtype=jnp.int32)
    column_code = (columns // wide) * LANES_T + columns % LANES_T
    sel = (named[:, None] == column_code[None, :]).astype(jnp.float32)
    group = ((columns % wide) // LANES_T)[:, None] == jnp.arange(128, dtype=jnp.int32)[None, :]
    live = (jnp.arange(KT, dtype=jnp.int32)[None, :] < tile_count[:, None]).reshape(slot_count)
    mine = (order // KT)[None, :] == jnp.arange(stations, dtype=jnp.int32)[:, None]
    hits = (mine & live[None, :])[:, :, None] & (place[None, :, None] == jnp.arange(INNER * slots, dtype=jnp.int32)[None, None, :])
    weights = jnp.sum(hits.astype(jnp.float32), axis=1)
    weights2 = jnp.sum(((mine & live[None, :])[:, None, :] & in_group[None]).astype(jnp.float32), axis=2)

    ext = rows + 2 * ITERS
    vmem = pl.BlockSpec(memory_space=pltpu.VMEM)
    dma = pltpu.SemaphoreType.DMA
    observed = pl.pallas_call(
        functools.partial(kernel, outer_n, slots, splits),
        out_shape=jax.ShapeDtypeStruct((stations, 128), jnp.float32),
        in_specs=[pl.BlockSpec(memory_space=pltpu.SMEM)] + [vmem] * 10,
        out_specs=vmem,
        scratch_shapes=[
            pltpu.VMEM((INNER * slots, footprint.shape[2]), jnp.bfloat16),
            pltpu.VMEM((INNER * slots, footprint.shape[2]), jnp.bfloat16),
            pltpu.VMEM((INNER * GROUP_ROWS, footprint.shape[2] // splits), jnp.bfloat16),
            pltpu.VMEM((INNER * GROUP_ROWS, footprint.shape[2] // splits), jnp.bfloat16),
            pltpu.VMEM((2, ITERS, wide, TILE_LON), jnp.bfloat16),
            pltpu.VMEM((2, ITERS, LANES_T, TILE_LON), jnp.float32),
            pltpu.VMEM((ext, wide, TILE_LON), jnp.float32),
            pltpu.VMEM((ext, wide, TILE_LON), jnp.float32),
            pltpu.VMEM((ext, LANES_T, TILE_LON), jnp.float32),
            pltpu.VMEM((rows, outer_n * wide, TILE_LON), jnp.bfloat16),
            pltpu.VMEM((INNER * slots, outer_n * wide), jnp.float32),
            pltpu.VMEM((INNER * slots, 128), jnp.float32),
            pltpu.VMEM((INNER * slots, 128), jnp.float32),
            pltpu.VMEM((INNER * GROUP_ROWS, 128), jnp.float32),
            pltpu.VMEM((INNER * GROUP_ROWS, 128), jnp.float32),
            dma((INNER, PIECES)), dma((INNER, PIECES)),
            dma((INNER,)), dma((INNER,)),
            dma((2, 2)), dma((2, 2)),
            dma((outer_n - 1, PIECES)), dma((outer_n - 1, PIECES)),
            dma((outer_n - 1, PIECES)), dma((outer_n - 1, PIECES)),
            dma((INNER,)), dma((INNER,)),
            dma((INNER,)), dma((INNER,)),
        ],
        compiler_params=pltpu.CompilerParams(
            collective_id=0, has_side_effects=True, vmem_limit_bytes=50 * 1024 * 1024
        ),
    )(
        diff_steps, footprint, hot.astype(jnp.bfloat16),
        hot2.astype(jnp.bfloat16), flux_t, coef_t, sel, sel2.astype(jnp.float32), group.astype(jnp.float32),
        weights, weights2,
    )
    return lax.all_gather(observed[:, :samples], "sample", axis=1, tiled=True)


def solution(mesh):
    in_specs = (
        P("sample", "station", None),
        P("station", None),
        P("sample"),
        P("station", None, None),
        P(),
        P(),
        P("station"),
    )
    out_specs = P("station", None)
    return jax.shard_map(body, mesh=mesh, in_specs=in_specs, out_specs=out_specs, check_vma=False)
```

profile of v0, /device:TPU:0, one launch (start us, length us, event | category | flops | bytes accessed | tf_op | source)
XLA Modules:
  0.0 98.2 jit_solution(11544204219404913603)
XLA Ops:
  0.0 0.7 bitcast_add_fusion
  0.7 0.1 copy.18
  0.9 0.2 reshape.494
  1.2 0.4 convert_reduce_fusion.2
  1.7 0.1 compare_and_fusion
  1.8 0.0 copy-start.1
  1.8 0.1 copy.21.hot2
  2.0 2.2 %reshape.495 = bf16[4,32,7,512]{3,2,1,0:T(8,128)(2,1)S(1)} reshape(bf16[4,32,3584]{2,1,0:T(8,128)(2,1)} %param.7) | data formatting | bytes 1835008 | tf_op jit(solution)/shard_map/reshape | solution.py:383
  4.1 0.0 copy-start.2
  4.2 0.0 copy-start
  4.2 0.2 pad_bitcast_fusion.flux
  4.4 0.0 copy-done.1
  4.4 0.2 reshape.497
  4.7 0.2 select_reduce_fusion
  4.9 0.1 sub.60
  5.0 0.1 compare_convert_fusion.sel
  5.1 0.1 select_reduce_fusion.1
  5.3 0.1 copy.20
  5.4 0.1 eq.297
  5.5 0.1 broadcast_compare_fusion
  5.6 0.1 and_convert_fusion.sel2
  5.7 0.1 fusion.2.group
  5.8 0.1 iota_compare_fusion.3
  5.9 0.0 copy-done.2
  5.9 0.1 iota_compare_fusion.6
  6.0 0.1 lt.142
  6.1 0.2 convert_reduce_fusion.1.weights
  6.3 0.2 convert_reduce_fusion.weights2
  6.6 0.0 copy-done
  6.6 91.0 %shard_map.73 = f32[16,128]{1,0:T(8,128)S(1)} custom-call(s32[4]{0:T(128)S(1)} %copy-done, bf16[16,4,16384]{2,1,0:T(4,128)(2,1)} %prints.1, bf16[128,64]{1,0:T(8,128)(2,1)S(1)} %fusion.hot, bf16[128,256]{1,0:T(8,128)(2,1)S(1)} %copy.21.hot2, bf16[32,32,512]{2,1,0:T(8,128)(2,1)S(1)} %pad_bitcast_fusion.flux, f32[32,8,512]{2,1,0:T(8,128)S(1)} %pad.9.coef, ...), custom_call_target="tpu_custom_call" | custom-call | tf_op jit(solution)/shard_map/pallas_call | solution.py:436
  97.6 0.7 copy.22
  (20 shorter events, 0.3 us)
Async XLA Ops:
  1.8 2.6 %copy-start.1 = (f32[32,3584]{1,0:T(8,128)S(1)}, f32[32,3584]{1,0:T(8,128)}, u32[]{:S(2)}) copy-start(f32[32,3584]{1,0:T(8,128)} %param.8) | copy-start | bytes 1376260
  4.1 1.8 %copy-start.2 = (s32[16]{0:T(128)S(1)}, s32[16]{0:T(128)}, u32[]{:S(2)}) copy-start(s32[16]{0:T(128)} %param.13) | copy-start | bytes 196
  4.2 2.4 %copy-start = (s32[4]{0:T(128)S(1)}, s32[4]{0:T(128)}, u32[]{:S(2)}) copy-start(s32[4]{0:T(128)} %steps.1) | copy-start | bytes 52
where the time goes:
time: 98.5 us; the launch traced here: 98.2 us
  Pallas kernels  91 us (92%)
  local copies, waits for them, and re-layouts  4.15 us (4%)
  other arithmetic  2.77 us (3%)
    pallas_call x1, Pallas kernels, body(): pl.pallas_call(functools.partial(kernel, outer_n, slots, splits), out_sha...  91 us
    reshape x1, local copies, waits for them, and re-layouts, body(): flux.reshape(samples, rows, TILES_DEV, TILE_LON).transpose(1, 0, 2, 3)  2.19 us

commit v1 on v0

--- a/solution.py
+++ b/solution.py
@@ -71,7 +71,10 @@
 
     for offset in range(1, INNER):
         greet(peer(offset))
-    others = ((lone_left, -INNER), (lone_right, INNER), (lone_up, -1), (lone_down, 1))
+    others = (
+        (lone_left, -INNER), (lone_right, INNER), (lone_up, -1), (lone_down, 1),
+        (first, 2 * INNER), (last, -2 * INNER), (outer == 2, -2 * INNER), (outer == outer_n - 3, 2 * INNER),
+    )
     for there, step in others:
         @pl.when(there)
         def _():
@@ -203,16 +206,18 @@
 
     piece = rows // PIECES
 
-    def block_copy(block, c, k, to_right):
+    def block_copy(block, c, k, to_right, hops=1):
         at = tiles.at[pl.ds(c * piece, piece), pl.ds(pl.multiple_of(block * wide, wide), wide), :]
         if to_right:
-            return remote(at, at, r_send.at[k, c], r_recv.at[k, c], me + INNER)
-        return remote(at, at, l_send.at[k, c], l_recv.at[k, c], me - INNER)
+            return remote(at, at, r_send.at[k, c], r_recv.at[k, c], me + hops * INNER)
+        return remote(at, at, l_send.at[k, c], l_recv.at[k, c], me - hops * INNER)
 
     def goes(there, k, to_right):
         there = jnp.logical_and(there, has_right if to_right else has_left)
         if k == 0:
             there = jnp.logical_and(there, outer != (outer_n - 2 if to_right else 1))
+        if k == 1:
+            there = jnp.logical_and(there, outer != (1 if to_right else outer_n - 2))
         return there
 
     def start_block(block, c, k, to_right, there):
@@ -234,6 +239,10 @@
     def send_piece(c):
         start_block(outer, c, 0, True, has_right)
         start_block(outer, c, 0, False, has_left)
+        for at_end, to_right in ((first, True), (last, False)):
+            @pl.when(at_end)
+            def _():
+                block_copy(outer, c, 1, to_right, 2).start()
 
     for k in range(ITERS):
         def row_pair(i, carry, k=k):
@@ -347,6 +356,12 @@
         out[...] += jnp.dot(weights2[...], ret2[...], precision=lax.Precision.HIGHEST, preferred_element_type=jnp.float32)
         for offset in range(INNER):
             group_copy(offset).wait_send()
+
+    for at_end, to_right in ((first, True), (last, False)):
+        @pl.when(at_end)
+        def _():
+            for c in range(PIECES):
+                block_copy(outer, c, 1, to_right, 2).wait_send()
 
     @pl.when(is_next)
     def _():

time: 98.5 us -> 101 us (1.025)
  Pallas kernels: 91 us -> 93.9 us
    pallas_call x1, Pallas kernels: 91 us -> 93.9 us  [body(): pl.pallas_call(functools.partial(kernel, outer_n, slots, splits), out_sha...]
where the time goes in v1:
time: 101 us
  Pallas kernels  93.9 us (93%)
  local copies, waits for them, and re-layouts  4.15 us (4%)
  other arithmetic  2.77 us (3%)
    pallas_call x1, Pallas kernels, body(): pl.pallas_call(functools.partial(kernel, outer_n, slots, splits), out_sha...  93.9 us
    reshape x1, local copies, waits for them, and re-layouts, body(): flux.reshape(samples, rows, TILES_DEV, TILE_LON).transpose(1, 0, 2, 3)  2.19 us

profile of v1, /device:TPU:0, one launch (start us, length us, event | category | flops | bytes accessed | tf_op | source)
XLA Modules:
  0.0 101.2 jit_solution(5427084792161689105)
XLA Ops:
  0.0 0.7 bitcast_add_fusion
  0.7 0.1 copy.18
  0.9 0.2 reshape.494
  1.2 0.4 convert_reduce_fusion.2
  1.7 0.1 compare_and_fusion
  1.8 0.0 copy-start.1
  1.8 0.1 copy.21.hot2
  2.0 2.2 %reshape.495 = bf16[4,32,7,512]{3,2,1,0:T(8,128)(2,1)S(1)} reshape(bf16[4,32,3584]{2,1,0:T(8,128)(2,1)} %param.7) | data formatting | bytes 1835008 | tf_op jit(solution)/shard_map/reshape | solution.py:398
  4.1 0.0 copy-start.2
  4.2 0.0 copy-start
  4.2 0.2 pad_bitcast_fusion.flux
  4.4 0.0 copy-done.1
  4.4 0.2 reshape.497
  4.7 0.2 select_reduce_fusion
  4.9 0.1 sub.60
  5.0 0.1 compare_convert_fusion.sel
  5.1 0.1 select_reduce_fusion.1
  5.3 0.1 copy.20
  5.4 0.1 eq.297
  5.5 0.1 broadcast_compare_fusion
  5.6 0.1 and_convert_fusion.sel2
  5.7 0.1 fusion.2.group
  5.8 0.1 iota_compare_fusion.3
  5.9 0.0 copy-done.2
  5.9 0.1 iota_compare_fusion.6
  6.0 0.1 lt.142
  6.1 0.2 convert_reduce_fusion.1.weights
  6.3 0.2 convert_reduce_fusion.weights2
  6.6 0.0 copy-done
  6.6 93.9 %shard_map.73 = f32[16,128]{1,0:T(8,128)S(1)} custom-call(s32[4]{0:T(128)S(1)} %copy-done, bf16[16,4,16384]{2,1,0:T(4,128)(2,1)} %prints.1, bf16[128,64]{1,0:T(8,128)(2,1)S(1)} %fusion.hot, bf16[128,256]{1,0:T(8,128)(2,1)S(1)} %copy.21.hot2, bf16[32,32,512]{2,1,0:T(8,128)(2,1)S(1)} %pad_bitcast_fusion.flux, f32[32,8,512]{2,1,0:T(8,128)S(1)} %pad.9.coef, ...), custom_call_target="tpu_custom_call" | custom-call | tf_op jit(solution)/shard_map/pallas_call | solution.py:451
  100.5 0.7 copy.22
  (20 shorter events, 0.3 us)
Async XLA Ops:
  1.8 2.6 %copy-start.1 = (f32[32,3584]{1,0:T(8,128)S(1)}, f32[32,3584]{1,0:T(8,128)}, u32[]{:S(2)}) copy-start(f32[32,3584]{1,0:T(8,128)} %param.8) | copy-start | bytes 1376260
  4.1 1.8 %copy-start.2 = (s32[16]{0:T(128)S(1)}, s32[16]{0:T(128)}, u32[]{:S(2)}) copy-start(s32[16]{0:T(128)} %param.13) | copy-start | bytes 196
  4.2 2.4 %copy-start = (s32[4]{0:T(128)S(1)}, s32[4]{0:T(128)}, u32[]{:S(2)}) copy-start(s32[4]{0:T(128)} %steps.1) | copy-start | bytes 52

commit v2 on v0

--- a/solution.py
+++ b/solution.py
@@ -274,15 +274,16 @@
             for j in range(piece):
                 step_row(c * piece + 2 * ITERS - 1 - k + j, k)
         send_piece(c)
-        relay(c - 1, 0)
-        relay(c - 2, 1, c >= 2)
+        relay(c - 2, 0, c >= 2)
+        relay(c - 4, 1, c >= 4)
         send_prints(c)
         return carry
 
     lax.fori_loop(1, PIECES, next_piece, 0)
-    relay(PIECES - 1, 0)
-    relay(PIECES - 2, 1)
-    relay(PIECES - 1, 1)
+    for c in range(PIECES - 2, PIECES):
+        relay(c, 0)
+    for c in range(PIECES - 4, PIECES):
+        relay(c, 1)
     arr[own, :] = send[own, :]
 
     def multiply(c):

time: 98.5 us -> 98.5 us (level)
  no operation moved by 1% of the time
where the time goes in v2:
time: 98.5 us; the launch traced here: 98.2 us
  Pallas kernels  91 us (92%)
  local copies, waits for them, and re-layouts  4.15 us (4%)
  other arithmetic  2.77 us (3%)
    pallas_call x1, Pallas kernels, body(): pl.pallas_call(functools.partial(kernel, outer_n, slots, splits), out_sha...  91 us
    reshape x1, local copies, waits for them, and re-layouts, body(): flux.reshape(samples, rows, TILES_DEV, TILE_LON).transpose(1, 0, 2, 3)  2.19 us

profile of v2, /device:TPU:0, one launch (start us, length us, event | category | flops | bytes accessed | tf_op | source)
XLA Modules:
  0.0 98.2 jit_solution(8315870610327813917)
XLA Ops:
  0.0 0.7 bitcast_add_fusion
  0.7 0.1 copy.18
  0.9 0.2 reshape.494
  1.2 0.4 convert_reduce_fusion.2
  1.7 0.1 compare_and_fusion
  1.8 0.0 copy-start.1
  1.8 0.1 copy.21.hot2
  2.0 2.2 %reshape.495 = bf16[4,32,7,512]{3,2,1,0:T(8,128)(2,1)S(1)} reshape(bf16[4,32,3584]{2,1,0:T(8,128)(2,1)} %param.7) | data formatting | bytes 1835008 | tf_op jit(solution)/shard_map/reshape | solution.py:384
  4.1 0.0 copy-start.2
  4.2 0.0 copy-start
  4.2 0.2 pad_bitcast_fusion.flux
  4.4 0.0 copy-done.1
  4.4 0.2 reshape.497
  4.7 0.2 select_reduce_fusion
  4.9 0.1 sub.60
  5.0 0.1 compare_convert_fusion.sel
  5.1 0.1 select_reduce_fusion.1
  5.3 0.1 copy.20
  5.4 0.1 eq.297
  5.5 0.1 broadcast_compare_fusion
  5.6 0.1 and_convert_fusion.sel2
  5.7 0.1 fusion.2.group
  5.8 0.1 iota_compare_fusion.3
  5.9 0.0 copy-done.2
  5.9 0.1 iota_compare_fusion.6
  6.0 0.1 lt.142
  6.1 0.2 convert_reduce_fusion.1.weights
  6.3 0.2 convert_reduce_fusion.weights2
  6.6 0.0 copy-done
  6.6 91.0 %shard_map.73 = f32[16,128]{1,0:T(8,128)S(1)} custom-call(s32[4]{0:T(128)S(1)} %copy-done, bf16[16,4,16384]{2,1,0:T(4,128)(2,1)} %prints.1, bf16[128,64]{1,0:T(8,128)(2,1)S(1)} %fusion.hot, bf16[128,256]{1,0:T(8,128)(2,1)S(1)} %copy.21.hot2, bf16[32,32,512]{2,1,0:T(8,128)(2,1)S(1)} %pad_bitcast_fusion.flux, f32[32,8,512]{2,1,0:T(8,128)S(1)} %pad.9.coef, ...), custom_call_target="tpu_custom_call" | custom-call | tf_op jit(solution)/shard_map/pallas_call | solution.py:437
  97.6 0.7 copy.22
  (20 shorter events, 0.3 us)
Async XLA Ops:
  1.8 2.6 %copy-start.1 = (f32[32,3584]{1,0:T(8,128)S(1)}, f32[32,3584]{1,0:T(8,128)}, u32[]{:S(2)}) copy-start(f32[32,3584]{1,0:T(8,128)} %param.8) | copy-start | bytes 1376260
  4.1 1.8 %copy-start.2 = (s32[16]{0:T(128)S(1)}, s32[16]{0:T(128)}, u32[]{:S(2)}) copy-start(s32[16]{0:T(128)} %param.13) | copy-start | bytes 196
  4.2 2.4 %copy-start = (s32[4]{0:T(128)S(1)}, s32[4]{0:T(128)}, u32[]{:S(2)}) copy-start(s32[4]{0:T(128)} %steps.1) | copy-start | bytes 52
